TPU v7x, 128 devices: a whole 4x4x4 slice. The times are simulated.
128 devices in a mesh: seq: 8 (over x, z_hi), chan: 16 (over y, z_lo, core).
Axes of the slice: x: 4, y: 4, z: 4 (z_hi: 2, z_lo: 2; z = z_hi * 2 + z_lo), core: 2. Of those that a mesh axis runs over, the one named last changes fastest.
Arguments:
- streams: bfloat16 [3, 16384, 8192], P(None, 'seq', 'chan'), may hold values from -6 to 6
- short_taps: float32 [3, 7, 8192], P(None, None, 'chan'), may hold values from -2.4 to 2.4
- rates: float32 [8192, 16], P('chan'), may hold values from 6.1035156e-06 to 0.05, as said below
- residues: float32 [8192, 16], P('chan'), may hold values from -1.5 to 1.5
- out_weight: bfloat16 [8192, 8192], P('chan'), may hold values from -0.09375 to 0.09375
Outputs:
- output: bfloat16 [16384, 8192], P('seq', 'chan')
Inputs may be any that keep to these rules, and one draw needn't show every extreme that they name: Every decay rate is positive and at most 0.05, so every mode decays and 1 - exp(-2 rates) is positive.
All inputs are finite; a program needn't handle non-finite values.
Results may differ from a plain program's by a relative error of at most 0.023.
Values may be sent and summed in bfloat16 or wider, within the bound.
A program may use at most 192 MiB of HBM per device.

v0:
```python
import jax
import jax.numpy as jnp
from jax import lax
from jax.sharding import PartitionSpec as P


def passed_along(value, axis, steps):
    count = lax.axis_size(axis)
    leading, last = (max(0, -steps), min(count, count - steps))
    return lax.ppermute(value, axis, [(source, source + steps) for source in range(leading, last)])


def decayed_prefix(contrib, rates, step):
    nblocks = contrib.shape[0]
    flat = contrib.reshape(nblocks, -1)
    features = flat.shape[1]
    rate_flat = (rates * step).reshape(-1)
    inner = 16
    outer = nblocks // inner
    lags = (
        jnp.arange(inner, dtype=jnp.int32)[:, None] - jnp.arange(inner, dtype=jnp.int32)[None, :]
    ).astype(rates.dtype)
    table = jnp.where(
        lags[:, :, None] >= 0,
        jnp.exp(-rate_flat[None, None, :] * jnp.maximum(lags, 0.0)[:, :, None]),
        jnp.zeros((), rates.dtype),
    )
    grid = flat.reshape(outer, inner, features)
    local = jnp.einsum("ijf,gjf->gif", table, grid, precision=lax.Precision.HIGHEST)
    totals = local[:, -1, :]
    glags = (
        jnp.arange(outer, dtype=jnp.int32)[:, None]
        - 1
        - jnp.arange(outer, dtype=jnp.int32)[None, :]
    ).astype(rates.dtype)
    gtable = jnp.where(
        glags[:, :, None] >= 0,
        jnp.exp(-rate_flat[None, None, :] * inner * jnp.maximum(glags, 0.0)[:, :, None]),
        jnp.zeros((), rates.dtype),
    )
    before = jnp.einsum("ghf,hf->gf", gtable, totals, precision=lax.Precision.HIGHEST)
    steps_in = (jnp.arange(inner, dtype=jnp.int32) + 1).astype(rates.dtype)
    carry_in = jnp.exp(-rate_flat[None, :] * steps_in[:, None])
    local = local + carry_in[None, :, :] * before[:, None, :]
    return local.reshape(contrib.shape)


def channel_major_mix(values, rates, residues, block_rows):
    channels, row_count = values.shape
    nblocks = row_count // block_rows
    positions = jnp.arange(block_rows).astype(rates.dtype)
    blocks = values.reshape(channels, nblocks, block_rows)
    inward = jnp.exp(-rates[:, :, None] * (block_rows - 1 - positions))
    contrib = jnp.einsum("cbt,cmt->bcm", blocks, inward, precision=lax.Precision.HIGHEST)
    inclusive = decayed_prefix(contrib, rates, block_rows)
    weights = residues * jnp.sqrt(-jnp.expm1(-2.0 * rates))
    powers = jnp.exp(-rates[:, :, None] * positions)
    kernel = jnp.einsum("cm,cmt->ct", weights, powers, precision=lax.Precision.HIGHEST)
    lag_table = (
        jnp.arange(block_rows, dtype=jnp.int32)[:, None]
        - jnp.arange(block_rows, dtype=jnp.int32)[None, :]
    )
    toeplitz = jnp.where(
        lag_table >= 0, kernel[:, jnp.maximum(lag_table, 0)], jnp.zeros((), rates.dtype)
    )
    intra_part = jnp.einsum("cts,cbs->cbt", toeplitz, blocks, precision=lax.Precision.HIGHEST)
    states = jnp.concatenate([jnp.zeros_like(inclusive[:1]), inclusive[:-1]], axis=0)
    outward = weights[:, :, None] * jnp.exp(-rates[:, :, None] * (positions + 1.0))
    inter_part = jnp.einsum("bcm,cmt->cbt", states, outward, precision=lax.Precision.HIGHEST)
    return (intra_part + inter_part).reshape(channels, row_count)


def on_device(streams, short_taps, rates, residues, out_weight):
    tap_count = short_taps.shape[1]
    margin = tap_count - 1
    row_count = streams.shape[1]
    local_width = streams.shape[2]
    margin_rows = passed_along(streams[:, row_count - margin :, :], "seq", 1)
    extended = jnp.concatenate([margin_rows, streams], axis=1).astype(jnp.float32)
    filtered = jnp.zeros((3, row_count, local_width), jnp.float32)
    for offset in range(tap_count):
        filtered = (
            filtered
            + short_taps[:, offset, None, :]
            * extended[:, margin - offset : margin - offset + row_count, :]
        )
    product = (filtered[1] * filtered[2]).astype(jnp.bfloat16)
    moved = lax.all_to_all(product.T, "seq", split_axis=0, concat_axis=1, tiled=True)
    col_width = moved.shape[0]
    first_col = lax.axis_index("seq") * col_width
    my_rates = lax.dynamic_slice_in_dim(rates, first_col, col_width, 0)
    my_residues = lax.dynamic_slice_in_dim(residues, first_col, col_width, 0)
    values = moved.astype(jnp.float32)
    block_rows = min(128, values.shape[1])
    mixed_cols = channel_major_mix(values, my_rates, my_residues, block_rows).astype(jnp.bfloat16)
    mixed_rows = lax.all_to_all(mixed_cols, "seq", split_axis=1, concat_axis=0, tiled=True).T
    gated_rows = (filtered[0] * mixed_rows.astype(jnp.float32)).astype(jnp.bfloat16)
    summed = lax.psum_scatter(
        lax.dot_general(
            out_weight, gated_rows, (((0,), (1,)), ((), ())), preferred_element_type=jnp.float32
        ).astype(jnp.bfloat16),
        "chan",
        scatter_dimension=0,
        tiled=True,
    ).astype(jnp.float32)
    return summed.T.astype(jnp.bfloat16)


def solution(mesh):
    return jax.shard_map(
        on_device,
        mesh=mesh,
        in_specs=(
            P(None, "seq", "chan"),
            P(None, None, "chan"),
            P("chan", None),
            P("chan", None),
            P("chan", None),
        ),
        out_specs=P("seq", "chan"),
        check_vma=False,
    )
```

profile of v0, /device:TPU:1, one launch (start us, length us, event | category | flops | bytes accessed | tf_op | source)
XLA Modules:
  0.0 636.7 jit_solution(14033294641484026045)
XLA Ops:
  6.5 0.7 slice.61
  7.5 6.4 collective-permute-start
  13.9 0.8 sqrt_multiply_fusion
  14.9 1.2 fusion.42
  16.2 0.3 multiply_reduce_fusion
  16.5 8.8 %copy.25 = bf16[3,2048,512]{1,2,0:T(8,128)(2,1)} copy(bf16[3,2048,512]{2,1,0:T(8,128)(2,1)} %param.5) | data formatting | bytes 12582912 | tf_op args[0]
  25.4 10.4 %maximum_convert_fusion = f32[3,2054,512]{1,2,0:T(8,128)} fusion(bf16[3,2048,512]{1,2,0:T(8,128)(2,1)} %copy.25, bf16[3,6,512]{1,2,0:T(8,128)(2,1)S(1)} %collective-permute-done), kind=kLoop, calls=%fused_computation.19 | loop fusion | flops 12619776 | bytes 18929664 | tf_op jit(solution)/shard_map/convert_element_type | solution.py:79
  35.8 38.9 %fusion = f32[3,2048,512]{1,2,0:T(8,128)} fusion(f32[3,2054,512]{1,2,0:T(8,128)} %maximum_convert_fusion, f32[3,512]{1,0:T(4,128)S(1)} %get-tuple-element.15, f32[3,512]{1,0:T(4,128)S(1)} %get-tuple-element.16, f32[3,512]{1,0:T(4,128)S(1)} %get-tuple-element.17, f32[3,512]{1,0:T(4,128)S(1)} %get-tuple-element.18, f32[3,512]{1,0:T(4,128)S(1)} %get-tuple-element.19, ...), kind=kLoop, calls=%fused_computation.3 | loop fusion | flops 40894464 | bytes 100706304 | tf_op jit(solution)/shard_map/add | solution.py:83
  74.7 5.4 fusion.10
  80.1 4.0 all-to-all-start
  84.1 11.5 %reduce-scatter.2.cloned.1.call-start = ((), (), s32[]{:S(2)}) async-start(), calls=%async_computation.3 | async-start | bytes 35651584 | tf_op jit(solution)/shard_map/reduce_scatter | solution.py:98
  96.2 54.8 %gather_fusion = f32[16384,64]{1,0:T(8,128)} fusion(f32[64,128]{0,1:T(8,128)S(1)} %copy.41, s32[16384]{0:T(1024)S(1)} %bitcast_clamp_fusion), kind=kCustom, calls=%fused_computation | custom fusion | bytes 8454144 | tf_op jit(solution)/shard_map/gather | solution.py:64
  151.0 7.4 %copy.28 = f32[128,128,64]{1,0,2:T(8,128)} copy(f32[128,128,64]{2,1,0:T(8,128)} %bitcast.66) | data formatting | bytes 8388608 | tf_op jit(solution)/shard_map/gather | solution.py:64
  158.6 2.5 copy.26
  161.1 2.9 reshape.178
  164.0 3.4 convolution_bitcast_fusion
  167.4 2.5 reshape.194
  169.9 15.9 %fusion.22 = f32[8,16,1024]{1,0,2:T(8,128)S(1)} fusion(f32[8,16,1024]{1,0,2:T(8,128)} %reshape.194, f32[16,16]{1,0:T(8,128)S(1)} %convert_maximum_fusion, f32[1024]{0:T(1024)S(1)} %neg.33, pred[16,16]{1,0:T(8,128)(4,1)S(1)} %convert_compare_fusion), kind=kOutput, calls=%fused_computation.34 | convolution fusion | flops 25690112 | bytes 1053952 | tf_op jit(solution)/shard_map/ijf,gjf->gif/dot_general | solution.py:29
  185.9 1.9 copy-done.1
  187.8 3.1 slice.92
  190.9 2.8 copy.61
  194.2 6.9 %multiply_add_fusion = f32[8,16,1024]{1,0,2:T(8,128)} fusion(f32[8,16,1024]{1,0,2:T(8,128)} %copy-done.1, f32[8,1024]{0,1:T(8,128)S(1)} %bitcast.69, f32[16,1024]{0,1:T(8,128)S(1)} %copy.32), kind=kLoop, calls=%fused_computation.29 | loop fusion | flops 262144 | bytes 1146880 | tf_op jit(solution)/shard_map/add | solution.py:44
  201.0 3.4 reshape.195
  204.5 7.1 %fusion.27 = f32[64,128,128]{2,1,0:T(8,128)S(1)} fusion(f32[127,64,16]{0,2,1:T(8,128)S(1)} %bitcast.68, f32[64,16]{1,0:T(8,128)S(1)} %copy.59, f32[128]{0:T(128)S(1)} %broadcast_add_fusion, f32[64,16]{1,0:T(8,128)S(1)} %copy.27), kind=kOutput, calls=%fused_computation.39 | convolution fusion | flops 201588736 | bytes 4723200 | tf_op jit(solution)/shard_map/bcm,cmt->cbt/dot_general | solution.py:69
  211.6 5.7 add_convert_fusion
  217.3 2.8 convert_element_type.99
  220.1 1.2 copy.37
  221.3 31.9 %all_to_all.26 = bf16[64,8,2048]{2,0,1:T(8,128)(2,1)S(1)} all-to-all(bf16[64,8,2048]{2,0,1:T(8,128)(2,1)S(1)} %copy.37), channel_id=1, replica_groups=mesh['seq'=8,'chan'=16] {'seq'}, dimensions={1} | all-to-all | bytes 4194304 | tf_op jit(solution)/shard_map/all_to_all | solution.py:96
  253.2 3.1 fusion.12
  256.3 0.4 slice-done.1
  256.6 21.7 %convert_bitcast_fusion = bf16[8192,2048]{0,1:T(8,128)(2,1)} fusion(bf16[2048,512]{0,1:T(8,128)(2,1)S(1)} %fusion.12, bf16[512,8192]{1,0:T(8,128)(2,1)S(1)} %bitcast.73), kind=kOutput, calls=%fused_computation.1 | convolution fusion | flops 17196646400 | bytes 44040192 | tf_op jit(solution)/shard_map/dot_general | solution.py:99
  278.4 351.0 %reduce-scatter.2.cloned.1.call-done = bf16[512,2048]{0,1:T(8,128)(2,1)} async-done(((bf16[8192,2048]{0,1:T(8,128)(2,1)}), bf16[512,2048]{0,1:T(8,128)(2,1)}) %reduce-scatter.2.cloned.1.call-update) | async-done | bytes 2097168 | tf_op jit(solution)/shard_map/reduce_scatter | solution.py:98
  (36 shorter events, 1.6 us)
Async XLA Ops:
  7.5 17.8 %collective-permute-start = (bf16[3,6,512]{1,2,0:T(8,128)(2,1)S(1)}, bf16[3,6,512]{1,2,0:T(8,128)(2,1)S(1)}, u32[]{:S(2)}, u32[]{:S(2)}) collective-permute-start(bf16[3,6,512]{1,2,0:T(8,128)(2,1)S(1)} %copy.24), channel_id=1, source_target_pairs={{0,16},{16,32},{32,48},{48,64},{64,80},{80,96},{96,112},{1,17},{17... | collective-permute-start | bytes 55304 | tf_op jit(solution)/shard_map/ppermute | solution.py:10
  80.1 78.5 %all-to-all-start = ((bf16[8,64,2048]{2,1,0:T(8,128)(2,1)}), bf16[8,64,2048]{2,1,0:T(8,128)(2,1)S(1)}, u32[]{:S(2)}, u32[]{:S(2)}) async-start(bf16[8,64,2048]{2,1,0:T(8,128)(2,1)} %bitcast.5), calls=%async_computation | async-start | bytes 4194304 | tf_op jit(solution)/shard_map/all_to_all | solution.py:88
  84.1 545.3 %reduce-scatter.2.cloned.1.call-start = ((), (), s32[]{:S(2)}) async-start(), calls=%async_computation.3 | async-start | bytes 35651584 | tf_op jit(solution)/shard_map/reduce_scatter | solution.py:98
  185.9 1.9 copy-start.1
  204.5 7.1 %copy-start = (f32[128,128,64]{1,0,2:T(8,128)S(1)}, f32[128,128,64]{1,0,2:T(8,128)}, u32[]{:S(2)}) copy-start(f32[128,128,64]{1,0,2:T(8,128)} %copy.28) | copy-start | bytes 12582916
  220.1 36.1 %slice-start = ((s8[8388608]{0:T(1024)(128)(4,1)}), s8[4194304]{0:T(1024)(128)(4,1)S(1)}, s32[]{:S(2)}) async-start(s8[8388608]{0:T(1024)(128)(4,1)} %bitcast.72), calls=%async_computation.4 | async-start | bytes 8388608
  253.2 3.4 slice-start.1
Sparse Core Ops, SparseCore 0:
  278.5 350.8 reduce-scatter.1
where the time goes:
time: 645 us; the launch traced here: 637 us
  waiting for transfers between devices  351 us (54%)
  local copies, waits for them, and re-layouts  97.6 us (15%)
  other arithmetic  66.4 us (10%)
  matrix products  53.9 us (8%)
  blocking collectives  31.9 us (5%)
  starting transfers between devices  21.8 us (3%)
  between operations  14.1 us (2%)
    reduce_scatter x1, waiting for transfers between devices, on_device(): lax.psum_scatter(lax.dot_general(out_weight, gated_rows, (((0,), (1,)), (...  351 us
    gather x2, local copies, waits for them, and re-layouts, channel_major_mix(): kernel[:, jnp.maximum(lag_table, 0)]  62.2 us
    add x1, other arithmetic, on_device(): filtered + short_taps[:, offset, None, :] * extended[:, margin - offset:m...  38.9 us
    all_to_all x1, blocking collectives, on_device(): lax.all_to_all(mixed_cols, 'seq', split_axis=1, concat_axis=0, tiled=True)  31.9 us
    dot_general x1, matrix products, on_device(): lax.dot_general(out_weight, gated_rows, (((0,), (1,)), ((), ())), preferr...  21.7 us
    dot_general x1, matrix products, decayed_prefix(): jnp.einsum('ijf,gjf->gif', table, grid, precision=lax.Precision.HIGHEST)  15.9 us
    unnamed x15, local copies, waits for them, and re-layouts  14.1 us
  transfers between devices with their start and end apart: 3, of which 1 were waited for; matrix products, arithmetic and copies ran while one was open for 12% of the time, Pallas kernels for 0%

commit v1 on v0

v1 whole, which is shorter than its diff:
```python
import functools

import jax
import jax.numpy as jnp
from jax import lax
from jax.experimental import pallas as pl
from jax.experimental.pallas import tpu as pltpu
from jax.sharding import PartitionSpec as P

MESH = pl.DeviceIdType.MESH
F32 = jnp.float32
BF16 = jnp.bfloat16

TAPS = 7
MODES = 16
ROWS = 2048
WIDTH = 512
LANES = 128
TILES = WIDTH // LANES
CHUNKS = 8
STEPS = ROWS // CHUNKS
WINDOWS = 8
WSTEPS = STEPS // WINDOWS
WROWS = ROWS // WINDOWS
HALF = WIDTH // 2
PAD = 8
ORDER = (2, 1, 3, 0)
SEQ = 8
XPART = WIDTH // 4

LAG_F, LAG_2, LAG_1, LAG_0 = 2, 2, 3, 5


def kernel(
    streams, taps, rates, gains, weight, out,
    sbuf, halo, nat, prod, query, state, decay, gain, total, totals, stage,
    gated, wbuf, relay_out, relay_in, side_out, side_in, result,
    load_sem, wown_sem, halo_sem, state_sem, wsib_sem, wz_sem, wx1_sem, wx2_sem,
    gz_sem, gs_sem, gf_sem, relay_sem, side_sem, result_sem,
):
    seq, chan = lax.axis_index("seq"), lax.axis_index("chan")
    x, zh = lax.div(seq, 2), lax.rem(seq, 2)
    y, zl, core = lax.div(chan, 4), lax.rem(lax.div(chan, 2), 2), lax.rem(chan, 2)
    mine = zl * 2 + core
    sib_chan = chan + 1 - 2 * core
    z_chan = chan + 2 - 4 * zl

    def chan_of(yy, zz, cc):
        return (yy * 2 + zz) * 2 + cc

    def y_off(k):
        return lax.rem(y + k, 4)

    sibling = (seq, sib_chan)
    z_near = (seq, z_chan)
    zh_seq = seq + 1 - 2 * zh
    z_far = tuple((zh_seq, chan_of(y, 1 - zl, c)) for c in range(2))
    y_up = (seq, chan_of(y_off(1), zl, core))
    y_down = (seq, chan_of(y_off(3), zl, core))
    x_up = (lax.rem(seq + 2, SEQ), chan)
    x_down = (lax.rem(seq + 6, SEQ), chan)
    seq_of = lambda k: (lax.rem(seq + k, SEQ), chan)

    def send(src, dst, sems, index, device):
        return pltpu.make_async_remote_copy(
            src_ref=src, dst_ref=dst, send_sem=sems.at[(0, *index)], recv_sem=sems.at[(1, *index)],
            device_id=device, device_id_type=MESH,
        )

    def load(j):
        return pltpu.make_async_copy(streams.at[j], sbuf.at[j], load_sem.at[j])

    def columns(block, zz, cc):
        return pl.ds(pl.multiple_of(chan_of(y_off(block), zz, cc) * WIDTH, WIDTH), WIDTH)

    def own_weight(block):
        rows = pl.ds(pl.multiple_of(mine * WIDTH, WIDTH), WIDTH)
        return pltpu.make_async_copy(
            weight.at[:, columns(block, zl, core)], wbuf.at[block, rows], wown_sem.at[block]
        )

    for j in (1, 2, 0):
        load(j).start()
    for block in ORDER:
        own_weight(block).start()

    barrier = pltpu.get_barrier_semaphore()
    partners = [seq_of(k) for k in range(1, SEQ)] + [sibling, z_near, *z_far, y_up, y_down]
    for device in partners:
        pl.semaphore_signal(barrier, inc=1, device_id=device, device_id_type=MESH)
    pl.semaphore_wait(barrier, len(partners))

    halo_copy = send(streams.at[:, pl.ds(ROWS - 16, 16)], halo, halo_sem, (), seq_of(1))
    halo_copy.start()

    def weight_far_from(block, c):
        rows = pl.ds(pl.multiple_of((2 - 2 * zl + c) * WIDTH + x * XPART, XPART), XPART)
        return send(wbuf.at[block, rows], wbuf.at[block, rows], wz_sem, (block, c), z_far[0])

    def weight_sib(block):
        rows = pl.ds(pl.multiple_of(mine * WIDTH, WIDTH), WIDTH)
        return send(
            weight.at[:, columns(block, zl, 1 - core)], wbuf.at[block, rows], wsib_sem, (block,), sibling
        )

    def weight_x(block, c, part, device, sems, index):
        rows = pl.ds(pl.multiple_of((2 - 2 * zl + c) * WIDTH + part * XPART, XPART), XPART)
        return send(wbuf.at[block, rows], wbuf.at[block, rows], sems, index, device)

    def weight_x1(block):
        return [
            weight_x(block, c, x, device, wx1_sem, (block, way, c))
            for c in range(2)
            for way, device in enumerate((x_up, x_down))
        ]

    def weight_x2(block):
        return [
            weight_x(block, 0, lax.rem(x + 3, 4), x_up, wx2_sem, (block, 0)),
            weight_x(block, 1, lax.rem(x + 1, 4), x_down, wx2_sem, (block, 1)),
        ]

    for block in ORDER:
        for c in range(2):
            rows = pl.ds(pl.multiple_of(mine * WIDTH + x * XPART, XPART), XPART)
            part = pl.ds(pl.multiple_of(x * XPART, XPART), XPART)
            pltpu.make_async_remote_copy(
                src_ref=weight.at[part, columns(block, 1 - zl, c)], dst_ref=wbuf.at[block, rows],
                send_sem=wz_sem.at[0, block, c], recv_sem=wz_sem.at[1, block, core],
                device_id=z_far[c], device_id_type=MESH,
            ).start()
        weight_sib(block).start()

    def pass_x1(block):
        for c in range(2):
            weight_far_from(block, c).wait_recv()
        for copy in weight_x1(block):
            copy.start()

    def pass_x2(block):
        for copy in weight_x1(block):
            copy.wait_recv()
        for copy in weight_x2(block):
            copy.start()

    def have_weight(block):
        for copy in weight_x2(block):
            copy.wait_recv()
        weight_sib(block).wait_recv()
        own_weight(block).wait()

    def lanes_of(tile):
        return pl.ds(pl.multiple_of(tile * LANES, LANES), LANES)

    @pl.loop(0, TILES)
    def _(tile):
        for m in range(MODES):
            rate = rates[pl.ds(m, 1), lanes_of(tile)]
            decay[tile, m] = jnp.broadcast_to(jnp.exp(-rate), (CHUNKS, LANES))
            gain[tile, m] = jnp.broadcast_to(gains[pl.ds(m, 1), lanes_of(tile)], (CHUNKS, LANES))

    first = jnp.where(seq > 0, 1.0, 0.0).astype(F32)

    def widen(j, tile, slot):
        lanes = lanes_of(tile)
        nat[slot, pl.ds(0, PAD)] = halo[j, :, lanes].astype(F32)[16 - PAD :] * first

        @pl.loop(0, ROWS // 128)
        def _(i):
            row = pl.multiple_of(i * 128, 128)
            nat[slot, pl.ds(pl.multiple_of(row + PAD, PAD), 128)] = sbuf[j, pl.ds(row, 128), lanes].astype(F32)

    def across(slot, step):
        return nat[slot, pl.ds(PAD + step, CHUNKS, stride=STEPS), :]

    def filtered(window, coefs):
        terms = [c * v for c, v in zip(coefs, window, strict=True)]
        while len(terms) > 1:
            terms = [a + b for a, b in zip(terms[::2], terms[1::2])] + ([terms[-1]] if len(terms) % 2 else [])
        return terms[0]

    def coefs_of(j, tile):
        return [
            jnp.broadcast_to(taps[j, pl.ds(i, 1), lanes_of(tile)], (CHUNKS, LANES)) for i in range(TAPS)
        ]

    def convolve(tile, pairs, target):
        coefs = [coefs_of(j, tile) for j, _ in pairs]
        before = [tuple(across(slot, -i) for i in range(1, TAPS)) for _, slot in pairs]

        def body(g, before):
            before = list(before)
            for u in range(8):
                step = g * 8 + u
                value = None
                for k, (_, slot) in enumerate(pairs):
                    window = (across(slot, step), *before[k])
                    part = filtered(window, coefs[k])
                    value = part if value is None else value * part
                    before[k] = window[:-1]
                target[tile, pl.ds(pl.multiple_of(step * CHUNKS, CHUNKS), CHUNKS)] = value
            return tuple(before)

        lax.fori_loop(0, STEPS // 8, body, tuple(before))

    load(1).wait()
    load(2).wait()
    halo_copy.wait_recv()

    @pl.loop(0, TILES)
    def _(tile):
        widen(1, tile, 0)
        widen(2, tile, 1)
        convolve(tile, ((1, 0), (2, 1)), prod)

    pass_x1(ORDER[0])

    sublane = lax.broadcasted_iota(jnp.int32, (CHUNKS, LANES), 0)

    @pl.loop(0, TILES)
    def _(tile):
        decays = [decay[tile, m] for m in range(MODES)]

        def body(g, states):
            states = list(states)
            for u in range(8):
                step = pl.multiple_of((g * 8 + u) * CHUNKS, CHUNKS)
                value = prod[tile, pl.ds(step, CHUNKS)]
                states = [a * s + value for a, s in zip(decays, states)]
            return tuple(states)

        zero = jnp.zeros((CHUNKS, LANES), F32)
        ends = lax.fori_loop(0, STEPS // 8, body, (zero,) * MODES)
        for m in range(MODES):
            rate = jnp.broadcast_to(rates[pl.ds(m, 1), lanes_of(tile)], (CHUNKS, LANES))
            run = ends[m]
            for shift in (1, 2, 4):
                moved = jnp.where(sublane >= shift, pltpu.roll(run, shift, 0), 0.0)
                run = run + jnp.exp(-rate * float(STEPS * shift)) * moved
            state[tile, m] = jnp.where(sublane >= 1, pltpu.roll(run, 1, 0), 0.0)
            total[pl.ds(m, 1), lanes_of(tile)] = run[CHUNKS - 1 :]

    def state_copy(k):
        return send(total, totals.at[k], state_sem, (k,), seq_of(k))

    for k in range(1, SEQ):
        state_copy(k).start()

    pass_x1(ORDER[1])

    load(0).wait()

    @pl.loop(0, TILES)
    def _(tile):
        widen(0, tile, 0)
        convolve(tile, ((0, 0),), query)

    pass_x2(ORDER[0])
    pass_x1(ORDER[2])

    for k in range(1, SEQ):
        state_copy(k).wait_recv()

    @pl.loop(0, TILES)
    def _(tile):
        lanes = lanes_of(tile)
        rate = rates[:, lanes]
        start = jnp.zeros((MODES, LANES), F32)
        for k in range(1, SEQ):
            part = jnp.exp(-rate * float(ROWS * (k - 1))) * totals[k, :, lanes]
            start = start + jnp.where(seq >= k, part, 0.0)
        for m in range(MODES):
            spread = jnp.broadcast_to(rate[m : m + 1], (CHUNKS, LANES)) * (sublane * STEPS).astype(F32)
            state[tile, m] = state[tile, m] + jnp.exp(-spread) * start[m : m + 1]

    def own_lanes():
        return pl.ds(pl.multiple_of(mine * WIDTH, WIDTH), WIDTH)

    def part_of(w, source):
        return gated.at[w, :, pl.ds(pl.multiple_of(source * WIDTH, WIDTH), WIDTH)]

    def to_near(w):
        return send(part_of(w, mine), part_of(w, mine), gz_sem, (w,), z_near)

    def to_sibling(w):
        return send(part_of(w, mine), part_of(w, mine), gs_sem, (w,), sibling)

    def forward(w):
        source = (1 - zl) * 2 + core
        return send(part_of(w, source), part_of(w, source), gf_sem, (w,), sibling)

    def make_gated(w):
        @pl.loop(0, TILES)
        def _(tile):
            decays = [decay[tile, m] for m in range(MODES)]
            weights = [gain[tile, m] for m in range(MODES)]

            def body(g, states):
                states = list(states)
                for u in range(8):
                    at = g * 8 + u
                    row = pl.ds(pl.multiple_of((w * WSTEPS + at) * CHUNKS, CHUNKS), CHUNKS)
                    value = prod[tile, row]
                    states = [a * s + value for a, s in zip(decays, states)]
                    mixed = filtered(states, weights)
                    stage[pl.ds(at, CHUNKS, stride=WSTEPS), :] = mixed * query[tile, row]
                return tuple(states)

            states = lax.fori_loop(0, WSTEPS // 8, body, tuple(state[tile, m] for m in range(MODES)))
            for m in range(MODES):
                state[tile, m] = states[m]
            lanes = pl.ds(pl.multiple_of(mine * WIDTH + tile * LANES, LANES), LANES)
            gated[w, :, lanes] = stage[...].astype(BF16)

        to_near(w).start()
        to_sibling(w).start()

    def dot(w, block, n):
        return jnp.dot(gated[w], wbuf[block, :, pl.ds(n * HALF, HALF)], preferred_element_type=F32)

    ups = (y_up, y_down)

    def relay(w, way):
        return send(relay_out.at[way, w], relay_in.at[way, w], relay_sem, (way, w), ups[way])

    def side(w, way, n):
        return send(side_out.at[way, w, n], side_in.at[way, w, n], side_sem, (way, w, n), ups[way])

    def store(w, n):
        rows = pl.ds(pl.multiple_of(w * WSTEPS, WSTEPS), WSTEPS)
        return pltpu.make_async_copy(
            result.at[w, n], out.at[:, rows, pl.ds(n * HALF, HALF)], result_sem.at[w, n]
        )

    def opposite(w):
        for way in range(2):
            relay_out[way, w] = dot(w, 2, way).astype(BF16)
            relay(w, way).start()

    def sides(w):
        for way, block in ((0, 1), (1, 3)):
            side_out[way, w, 1 - way] = dot(w, block, 1 - way).astype(BF16)
            side(w, way, 1 - way).start()
        for way, block in ((0, 1), (1, 3)):
            part = dot(w, block, way)
            relay(w, way).wait_recv()
            side_out[way, w, way] = (part + relay_in[way, w].astype(F32)).astype(BF16)
            side(w, way, way).start()

    def finish(w):
        for n in range(2):
            part = dot(w, 0, n)
            for way in range(2):
                side(w, way, n).wait_recv()
                part = part + side_in[way, w, n].astype(F32)
            result[w, n] = part.astype(BF16).reshape(CHUNKS, WSTEPS, HALF)
            store(w, n).start()

    @pl.loop(0, WINDOWS + LAG_0)
    def _(i):
        @pl.when((i >= LAG_F) & (i < WINDOWS + LAG_F))
        def _():
            w = i - LAG_F
            to_near(w).wait_recv()
            forward(w).start()

        @pl.when(i < WINDOWS)
        def _():
            make_gated(i)

        @pl.when(i == 0)
        def _():
            pass_x2(ORDER[1])
            pass_x1(ORDER[3])

        @pl.when(i == 1)
        def _():
            pass_x2(ORDER[2])

        @pl.when(i == 2)
        def _():
            have_weight(ORDER[0])

        @pl.when(i == 3)
        def _():
            pass_x2(ORDER[3])
            have_weight(ORDER[1])
            have_weight(ORDER[2])

        @pl.when(i == LAG_0)
        def _():
            have_weight(ORDER[3])

        @pl.when((i >= LAG_2) & (i < WINDOWS + LAG_2))
        def _():
            w = i - LAG_2
            to_sibling(w).wait_recv()
            forward(w).wait_recv()
            opposite(w)

        @pl.when((i >= LAG_1) & (i < WINDOWS + LAG_1))
        def _():
            sides(i - LAG_1)

        @pl.when(i >= LAG_0)
        def _():
            finish(i - LAG_0)

    halo_copy.wait_send()
    for k in range(1, SEQ):
        state_copy(k).wait_send()
    for block in ORDER:
        for c in range(2):
            pltpu.make_async_remote_copy(
                src_ref=weight.at[pl.ds(0, XPART), columns(block, 1 - zl, c)],
                dst_ref=wbuf.at[block, pl.ds(0, XPART)],
                send_sem=wz_sem.at[0, block, c], recv_sem=wz_sem.at[1, block, c],
                device_id=z_far[c], device_id_type=MESH,
            ).wait_send()
        weight_sib(block).wait_send()
        for copy in weight_x1(block) + weight_x2(block):
            copy.wait_send()

    @pl.loop(0, WINDOWS)
    def _(w):
        to_near(w).wait_send()
        to_sibling(w).wait_send()
        forward(w).wait_send()
        for way in range(2):
            relay(w, way).wait_send()
            for n in range(2):
                side(w, way, n).wait_send()
        for n in range(2):
            store(w, n).wait()


def on_device(streams, short_taps, rates, residues, out_weight):
    gains = residues * jnp.sqrt(-jnp.expm1(-2.0 * rates))
    dma = pltpu.SemaphoreType.DMA
    vmem = pl.BlockSpec(memory_space=pltpu.VMEM)
    hbm = pl.BlockSpec(memory_space=pl.ANY)
    result = pl.pallas_call(
        kernel,
        out_shape=jax.ShapeDtypeStruct((CHUNKS, STEPS, WIDTH), BF16),
        in_specs=[hbm, vmem, vmem, vmem, hbm],
        out_specs=hbm,
        scratch_shapes=[
            pltpu.VMEM((3, ROWS, WIDTH), BF16),
            pltpu.VMEM((3, 16, WIDTH), BF16),
            pltpu.VMEM((2, ROWS + PAD, LANES), F32),
            pltpu.VMEM((TILES, ROWS, LANES), F32),
            pltpu.VMEM((TILES, ROWS, LANES), F32),
            pltpu.VMEM((TILES, MODES, CHUNKS, LANES), F32),
            pltpu.VMEM((TILES, MODES, CHUNKS, LANES), F32),
            pltpu.VMEM((TILES, MODES, CHUNKS, LANES), F32),
            pltpu.VMEM((MODES, WIDTH), F32),
            pltpu.VMEM((SEQ, MODES, WIDTH), F32),
            pltpu.VMEM((WROWS, LANES), F32),
            pltpu.VMEM((WINDOWS, WROWS, 4 * WIDTH), BF16),
            pltpu.VMEM((4, 4 * WIDTH, WIDTH), BF16),
            pltpu.VMEM((2, WINDOWS, WROWS, HALF), BF16),
            pltpu.VMEM((2, WINDOWS, WROWS, HALF), BF16),
            pltpu.VMEM((2, WINDOWS, 2, WROWS, HALF), BF16),
            pltpu.VMEM((2, WINDOWS, 2, WROWS, HALF), BF16),
            pltpu.VMEM((WINDOWS, 2, CHUNKS, WSTEPS, HALF), BF16),
            dma((3,)),
            dma((4,)),
            dma((2,)),
            dma((2, SEQ)),
            dma((2, 4)),
            dma((2, 4, 2)),
            dma((2, 4, 2, 2)),
            dma((2, 4, 2)),
            dma((2, WINDOWS)),
            dma((2, WINDOWS)),
            dma((2, WINDOWS)),
            dma((2, 2, WINDOWS)),
            dma((2, 2, WINDOWS, 2)),
            dma((WINDOWS, 2)),
        ],
        compiler_params=pltpu.CompilerParams(
            collective_id=0, has_side_effects=True, vmem_limit_bytes=60 * 1024 * 1024
        ),
        cost_estimate=pl.CostEstimate(
            flops=2 * ROWS * WIDTH * 8192, bytes_accessed=16 * 1024 * 1024, transcendentals=0
        ),
        name="mixer",
    )(streams, short_taps, rates.T, gains.T, out_weight)
    return result.reshape(ROWS, WIDTH)


def solution(mesh):
    return jax.shard_map(
        on_device,
        mesh=mesh,
        in_specs=(
            P(None, "seq", "chan"),
            P(None, None, "chan"),
            P("chan", None),
            P("chan", None),
            P("chan", None),
        ),
        out_specs=P("seq", "chan"),
        check_vma=False,
    )
```

time: 645 us -> 131 us (0.20); the launches traced: 637 us -> 130 us
  waiting for transfers between devices: 351 us -> 0 us
  Pallas kernels: 0 us -> 126 us
  local copies, waits for them, and re-layouts: 97.6 us -> 3.05 us
  other arithmetic: 66.4 us -> 1.42 us
  matrix products: 53.9 us -> 0 us
  blocking collectives: 31.9 us -> 0 us
  starting transfers between devices: 21.8 us -> 0 us
  between operations: 14.1 us -> 0.01 us
    reduce_scatter x1 -> x0, waiting for transfers between devices: 351 us -> none  [on_device(): lax.psum_scatter(lax.dot_general(out_weight, gated_rows, (((0,), (1,)), (...]
    pallas_call x0 -> x1, Pallas kernels: none -> 126 us  [on_device(): pl.pallas_call(kernel, out_shape=jax.ShapeDtypeStruct((CHUNKS, STEPS, WID...]
    gather x2 -> x0, local copies, waits for them, and re-layouts: 62.2 us -> none  [channel_major_mix(): kernel[:, jnp.maximum(lag_table, 0)]]
    dot_general x5 -> x0, matrix products: 53.9 us -> none  [the longest x1 21.7 us: on_device(): lax.dot_general(out_weight, gated_rows, (((0,), (1,)), ((), ())), preferr...]
    add x3 -> x0, other arithmetic: 45.8 us -> none  [the longest x1 38.9 us: on_device(): filtered + short_taps[:, offset, None, :] * extended[:, margin - offset:m...]
    all_to_all x1 -> x0, blocking collectives: 31.9 us -> none  [on_device(): lax.all_to_all(mixed_cols, 'seq', split_axis=1, concat_axis=0, tiled=True)]
    convert_element_type x5 -> x0, other arithmetic: 18.9 us -> none  [the longest x1 10.4 us: on_device(): jnp.concatenate([margin_rows, streams], axis=1).astype(jnp.float32)]
    reduce_scatter x1 -> x0, starting transfers between devices: 11.5 us -> none  [on_device(): lax.psum_scatter(lax.dot_general(out_weight, gated_rows, (((0,), (1,)), (...]
  transfers between devices with their start and end apart: 3 -> 0, of which waited for: 1 -> 0; matrix products, arithmetic and copies ran while one was open for 12% -> 0% of each run, Pallas kernels for 0% -> 0%
where the time goes in v1:
time: 131 us; the launch traced here: 130 us
  Pallas kernels  126 us (96%)
  local copies, waits for them, and re-layouts  3.05 us (2%)
  other arithmetic  1.42 us (1%)
    pallas_call x1, Pallas kernels, on_device(): pl.pallas_call(kernel, out_shape=jax.ShapeDtypeStruct((CHUNKS, STEPS, WID...  126 us
    unnamed x1, local copies, waits for them, and re-layouts  3.05 us

profile of v1, /device:TPU:1, one launch (start us, length us, event | category | flops | bytes accessed | tf_op | source)
XLA Modules:
  0.0 130.4 jit_solution(14516131406266078995)
XLA Ops:
  0.0 1.4 %multiply_bitcast_fusion.gains = f32[16,512]{1,0:T(8,128)} fusion(f32[512,16]{0,1:T(8,128)} %param.8, f32[512,16]{0,1:T(8,128)} %param.7), kind=kLoop, calls=%fused_computation | loop fusion | flops 24576 | bytes 98304 | tf_op jit(solution)/shard_map/transpose | solution.py:488
  1.4 126.0 %mixer.1 = bf16[8,256,512]{2,1,0:T(8,128)(2,1)} custom-call(bf16[3,2048,512]{2,1,0:T(8,128)(2,1)} %streams.1, f32[3,7,512]{2,1,0:T(8,128)} %taps.1, f32[16,512]{1,0:T(8,128)} %bitcast.5, f32[16,512]{1,0:T(8,128)} %multiply_bitcast_fusion.gains, bf16[512,8192]{1,0:T(8,128)(2,1)} %weight.1), custom_call_target="tpu_custom_call" | custom-call | flops 17179869184 | bytes 16777216 | tf_op jit(solution)/shard_map/mixer/pallas_call | solution.py:442
  127.4 3.0 %copy.7 = bf16[2048,512]{1,0:T(8,128)(2,1)} copy(bf16[2048,512]{1,0:T(8,128)(2,1)} %bitcast.4) | data formatting | bytes 4194304

commit v2 on v1

v2 whole, which is shorter than its diff:
```python
import functools

import jax
import jax.numpy as jnp
from jax import lax
from jax.experimental import pallas as pl
from jax.experimental.pallas import tpu as pltpu
from jax.sharding import PartitionSpec as P

MESH = pl.DeviceIdType.MESH
F32 = jnp.float32
BF16 = jnp.bfloat16

TAPS = 7
MODES = 16
ROWS = 2048
WIDTH = 512
LANES = 128
TILES = WIDTH // LANES
CHUNKS = 8
STEPS = ROWS // CHUNKS
WINDOWS = 16
WSTEPS = STEPS // WINDOWS
WROWS = ROWS // WINDOWS
HALF = WIDTH // 2
UNROLL = 16
EARLY = 8
PAD = 8
PITCH = STEPS + PAD
SPITCH = WSTEPS + PAD
PIECES = (((2, None),), ((1, 1), (3, 0)), ((1, 0), (3, 1)), ((0, None),))
SEQ = 8
XPART = WIDTH // 4

LAG_F, LAG_2, LAG_1, LAG_0 = 2, 3, 5, 8


def kernel(
    streams, taps_in, rates_in, gains_in, weight, out,
    taps, rates, gains,
    sbuf, halo, nat, prod, query, state, decay, gain, total, totals, stage,
    gated, wbuf, relay_out, relay_in, side_out, side_in, result,
    small_sem, load_sem, out_sem, wown_sem, halo_sem, state_sem, wsib_sem, wz_sem, wx_sem,
    gz_sem, gs_sem, relay_sem, side_sem, result_sem,
):
    seq, chan = lax.axis_index("seq"), lax.axis_index("chan")
    x, zh = lax.div(seq, 2), lax.rem(seq, 2)
    y, zl, core = lax.div(chan, 4), lax.rem(lax.div(chan, 2), 2), lax.rem(chan, 2)
    mine = zl * 2 + core
    sib_chan = chan + 1 - 2 * core
    z_chan = chan + 2 - 4 * zl

    def chan_of(yy, zz, cc):
        return (yy * 2 + zz) * 2 + cc

    def y_off(k):
        return lax.rem(y + k, 4)

    sibling = (seq, sib_chan)
    z_near = (seq, z_chan)
    near = tuple((seq, chan_of(y, 1 - zl, c)) for c in range(2))
    zh_seq = seq + 1 - 2 * zh
    z_far = tuple((zh_seq, chan_of(y, 1 - zl, c)) for c in range(2))
    y_up = (seq, chan_of(y_off(1), zl, core))
    y_down = (seq, chan_of(y_off(3), zl, core))
    x_up = (lax.rem(seq + 2, SEQ), chan)
    x_down = (lax.rem(seq + 6, SEQ), chan)
    seq_of = lambda k: (lax.rem(seq + k, SEQ), chan)

    (HALO, STATE, WSIB, WZ, WX, NEAR, SIB, RELAY, SIDE) = range(9)

    def send(src, dst, kind, sem, device):
        return pltpu.make_async_remote_copy(
            src_ref=src, dst_ref=dst, send_sem=out_sem.at[kind], recv_sem=sem,
            device_id=device, device_id_type=MESH,
        )

    def arrived(ref, sem):
        send(ref, ref, 0, sem, sibling).wait_recv()

    def left(ref, kind):
        send(ref, ref, kind, halo_sem.at[0], sibling).wait_send()

    small = [
        pltpu.make_async_copy(a, b, small_sem.at[i])
        for i, (a, b) in enumerate(((rates_in, rates), (gains_in, gains), (taps_in, taps)))
    ]

    def load(j, tile):
        lanes = pl.ds(pl.multiple_of(tile * LANES, LANES), LANES)
        return pltpu.make_async_copy(streams.at[j, :, lanes], sbuf.at[j, :, lanes], load_sem.at[j, tile])

    def columns(block, n, zz, cc):
        first = chan_of(y_off(block), zz, cc) * WIDTH
        if n is None:
            return pl.ds(pl.multiple_of(first, WIDTH), WIDTH)
        return pl.ds(pl.multiple_of(first + n * HALF, HALF), HALF)

    def half(n):
        return slice(None) if n is None else pl.ds(n * HALF, HALF)

    def own_weight(block):
        return pltpu.make_async_copy(
            weight.at[:, columns(block, None, zl, core)], wbuf.at[block, mine], wown_sem.at[block]
        )

    barrier = pltpu.get_barrier_semaphore()
    partners = [seq_of(k) for k in range(1, SEQ)] + [sibling, *near, *z_far, y_up, y_down]
    for device in partners:
        pl.semaphore_signal(barrier, inc=1, device_id=device, device_id_type=MESH)
    for copy in small:
        copy.start()
    for tile in range(TILES):
        for j in (1, 2):
            load(j, tile).start()

    halo_copy = send(streams.at[:, pl.ds(ROWS - 16, 16)], halo, HALO, halo_sem.at[0], seq_of(1))

    pair = 2 * lax.rem(x, 2)
    far_sources = pl.ds(2 - 2 * zl, 2)

    def part_rows(part):
        return pl.ds(pl.multiple_of(part * XPART, XPART), XPART)

    def start_weight(piece):
        for block, n in PIECES[piece]:
            for link in range(2):
                chip = near if link == 1 and piece < 2 else z_far
                for c in range(2):
                    send(
                        weight.at[part_rows(pair + link), columns(block, n, 1 - zl, c)],
                        wbuf.at[block, mine, part_rows(pair + link), half(n)],
                        WZ, wz_sem.at[piece], chip[c],
                    ).start()

    def pass_weight(piece):
        arrived(wbuf.at[0, 0], wz_sem.at[piece])
        for block, n in PIECES[piece]:
            for way, device in enumerate((x_up, x_down)):
                there = wbuf.at[block, far_sources, part_rows(pair + way), half(n)]
                send(there, there, WX, wx_sem.at[piece], device).start()

    def have_weight(piece):
        arrived(wbuf.at[0, 0], wx_sem.at[piece])

    def near_weight(block):
        there = wbuf.at[block, mine]
        return send(weight.at[:, columns(block, None, zl, 1 - core)], there, WSIB, wsib_sem.at[block], sibling)

    def have_near_weight(block):
        arrived(wbuf.at[block, 0], wsib_sem.at[block])
        own_weight(block).wait()

    pl.semaphore_wait(barrier, len(partners))
    halo_copy.start()
    start_weight(0)
    for copy in small:
        copy.wait()

    def lanes_of(tile):
        return pl.ds(pl.multiple_of(tile * LANES, LANES), LANES)

    @pl.loop(0, TILES)
    def _(tile):
        for m in range(MODES):
            rate = rates[pl.ds(m, 1), lanes_of(tile)]
            decay[tile, m] = jnp.broadcast_to(jnp.exp(-rate), (CHUNKS, LANES))
            gain[tile, m] = jnp.broadcast_to(gains[pl.ds(m, 1), lanes_of(tile)], (CHUNKS, LANES))

    first = jnp.where(seq > 0, 1.0, 0.0).astype(F32)

    def edge(j, tile, slot):
        nat[slot, pl.ds(0, PAD)] = halo[j, :, lanes_of(tile)].astype(F32)[16 - PAD :] * first

    def widen(j, tile, slot):
        lanes = lanes_of(tile)
        nat[slot, pl.ds(PAD, STEPS)] = sbuf[j, pl.ds(0, STEPS), lanes].astype(F32)

        @pl.loop(1, CHUNKS)
        def _(c):
            row = pl.multiple_of(c * STEPS - 16, 16)
            to = pl.multiple_of(c * PITCH, PAD)
            nat[slot, pl.ds(to, PITCH)] = sbuf[j, pl.ds(row, STEPS + 16), lanes].astype(F32)[16 - PAD :]

    def across(slot, step):
        return nat[slot, pl.ds(PAD + step, CHUNKS, stride=PITCH), :]

    def filtered(window, coefs):
        terms = [c * v for c, v in zip(coefs, window, strict=True)]
        while len(terms) > 1:
            terms = [a + b for a, b in zip(terms[::2], terms[1::2])] + ([terms[-1]] if len(terms) % 2 else [])
        return terms[0]

    def coefs_of(j, tile):
        return [
            jnp.broadcast_to(taps[j, pl.ds(i, 1), lanes_of(tile)], (CHUNKS, LANES)) for i in range(TAPS)
        ]

    def convolve(tile, pairs, target, first_group, groups):
        coefs = [coefs_of(j, tile) for j, _ in pairs]
        before = [tuple(across(slot, first_group * 8 - i) for i in range(1, TAPS)) for _, slot in pairs]

        def body(g, before):
            before = list(before)
            for u in range(8):
                step = g * 8 + u
                value = None
                for k, (_, slot) in enumerate(pairs):
                    window = (across(slot, step), *before[k])
                    part = filtered(window, coefs[k])
                    value = part if value is None else value * part
                    before[k] = window[:-1]
                target[tile, pl.ds(pl.multiple_of(step * CHUNKS, CHUNKS), CHUNKS)] = value
            return tuple(before)

        lax.fori_loop(first_group, groups, body, tuple(before))

    @pl.loop(0, TILES)
    def _(tile):
        load(1, tile).wait()
        load(2, tile).wait()
        widen(1, tile, 2 * tile)
        widen(2, tile, 2 * tile + 1)

        for slot in range(2):
            nat[2 * tile + slot, pl.ds(0, PAD)] = jnp.zeros((PAD, LANES), F32)
        convolve(tile, ((1, 2 * tile), (2, 2 * tile + 1)), prod, 0, STEPS // 8)

        @pl.when(tile == 2)
        def _():
            start_weight(1)
            for block in (2, 1, 3, 0):
                near_weight(block).start()
                own_weight(block).start()

    for tile in range(TILES):
        load(0, tile).start()
    arrived(halo, halo_sem.at[0])

    @pl.loop(0, TILES)
    def _(tile):
        edge(1, tile, 2 * tile)
        edge(2, tile, 2 * tile + 1)
        convolve(tile, ((1, 2 * tile), (2, 2 * tile + 1)), prod, 0, 1)

    sublane = lax.broadcasted_iota(jnp.int32, (CHUNKS, LANES), 0)

    @pl.loop(0, TILES)
    def _(tile):
        decays = [decay[tile, m] for m in range(MODES)]

        def body(g, states):
            states = list(states)
            for u in range(8):
                step = pl.multiple_of((g * 8 + u) * CHUNKS, CHUNKS)
                value = prod[tile, pl.ds(step, CHUNKS)]
                states = [a * s + value for a, s in zip(decays, states)]
            return tuple(states)

        zero = jnp.zeros((CHUNKS, LANES), F32)
        ends = lax.fori_loop(0, STEPS // 8, body, (zero,) * MODES)
        for m in range(MODES):
            rate = jnp.broadcast_to(rates[pl.ds(m, 1), lanes_of(tile)], (CHUNKS, LANES))
            run = ends[m]
            for shift in (1, 2, 4):
                moved = jnp.where(sublane >= shift, pltpu.roll(run, shift, 0), 0.0)
                run = run + jnp.exp(-rate * float(STEPS * shift)) * moved
            state[tile, m] = jnp.where(sublane >= 1, pltpu.roll(run, 1, 0), 0.0)
            total[pl.ds(m, 1), lanes_of(tile)] = run[CHUNKS - 1 :]

        @pl.when(tile == 0)
        def _():
            pass_weight(0)

        @pl.when(tile == 1)
        def _():
            start_weight(2)

    for k in range(1, SEQ):
        send(total, totals.at[k], STATE, state_sem.at[k], seq_of(k)).start()

    @pl.loop(0, TILES)
    def _(tile):
        load(0, tile).wait()
        widen(0, tile, tile)
        edge(0, tile, tile)
        convolve(tile, ((0, tile),), query, 0, EARLY)

    pass_weight(1)
    start_weight(3)
    for k in range(1, SEQ):
        arrived(totals.at[k], state_sem.at[k])

    @pl.loop(0, TILES)
    def _(tile):
        lanes = lanes_of(tile)
        rate = rates[:, lanes]
        start = jnp.zeros((MODES, LANES), F32)
        for k in range(1, SEQ):
            part = jnp.exp(-rate * float(ROWS * (k - 1))) * totals[k, :, lanes]
            start = start + jnp.where(seq >= k, part, 0.0)
        for m in range(MODES):
            spread = jnp.broadcast_to(rate[m : m + 1], (CHUNKS, LANES)) * (sublane * STEPS).astype(F32)
            state[tile, m] = state[tile, m] + jnp.exp(-spread) * start[m : m + 1]

    def own_lanes():
        return pl.ds(pl.multiple_of(mine * WIDTH, WIDTH), WIDTH)

    def part_of(w, source):
        return gated.at[w, :, pl.ds(pl.multiple_of(source * WIDTH, WIDTH), WIDTH)]

    def to_near(w):
        return send(part_of(w, mine), part_of(w, mine), NEAR, gz_sem.at[w], z_near)

    def to_sibling(w):
        return send(part_of(w, mine), part_of(w, mine), SIB, gs_sem.at[w], sibling)

    def forward(w):
        source = (1 - zl) * 2 + core
        arrived(part_of(w, source), gz_sem.at[w])
        return send(part_of(w, source), part_of(w, source), SIB, gs_sem.at[w], sibling)

    def make_gated(w):
        @pl.loop(0, TILES)
        def _(tile):
            decays = [decay[tile, m] for m in range(MODES)]
            weights = [gain[tile, m] for m in range(MODES)]

            def body(g, states):
                states = list(states)
                for u in range(UNROLL):
                    at = g * UNROLL + u
                    row = pl.ds(pl.multiple_of((w * WSTEPS + at) * CHUNKS, CHUNKS), CHUNKS)
                    value = prod[tile, row]
                    states = [a * s + value for a, s in zip(decays, states)]
                    mixed = filtered(states, weights)
                    stage[pl.ds(at, CHUNKS, stride=SPITCH), :] = mixed * query[tile, row]
                return tuple(states)

            states = lax.fori_loop(0, WSTEPS // UNROLL, body, tuple(state[tile, m] for m in range(MODES)))
            for m in range(MODES):
                state[tile, m] = states[m]
            lanes = pl.ds(pl.multiple_of(mine * WIDTH + tile * LANES, LANES), LANES)
            for c in range(CHUNKS):
                rows = pl.ds(c * WSTEPS, WSTEPS)
                gated[w, rows, lanes] = stage[pl.ds(c * SPITCH, WSTEPS)].astype(BF16)

        to_near(w).start()
        to_sibling(w).start()

    def dot(w, block, n):
        columns = wbuf[block, :, :, half(n)]
        return jnp.dot(gated[w], columns.reshape(4 * WIDTH, -1), preferred_element_type=F32)

    ups = (y_up, y_down)

    def side(w, way, n):
        return send(side_out.at[way, w, n], side_in.at[way, w, n], SIDE, side_sem.at[w], ups[way])

    def store(w):
        rows = pl.ds(pl.multiple_of(w * WSTEPS, WSTEPS), WSTEPS)
        return pltpu.make_async_copy(result.at[w], out.at[:, rows], result_sem.at[0])

    def opposite(w):
        part = dot(w, 2, None).astype(BF16)
        for way in range(2):
            relay_out[way, w] = part[:, way * HALF : (way + 1) * HALF]
        for way in range(2):
            send(relay_out.at[way, w], relay_in.at[way, w], RELAY, relay_sem.at[w], ups[way]).start()

    def sides_own(w):
        parts = [dot(w, block, 1 - way).astype(BF16) for way, block in ((0, 1), (1, 3))]
        for way in range(2):
            side_out[way, w, 1 - way] = parts[way]
        for way in range(2):
            side(w, way, 1 - way).start()

    def sides_relayed(w):
        parts = [dot(w, block, way) for way, block in ((0, 1), (1, 3))]
        arrived(relay_in.at[:, w], relay_sem.at[w])
        for way in range(2):
            side_out[way, w, way] = (parts[way] + relay_in[way, w].astype(F32)).astype(BF16)
        for way in range(2):
            side(w, way, way).start()

    def finish(w):
        part = dot(w, 0, None)
        arrived(side_in.at[:, w], side_sem.at[w])
        for n in range(2):
            sides = side_in[0, w, n].astype(F32) + side_in[1, w, n].astype(F32)
            total = (part[:, n * HALF : (n + 1) * HALF] + sides).astype(BF16)
            result[w, :, :, n * HALF : (n + 1) * HALF] = total.reshape(CHUNKS, WSTEPS, HALF)
        store(w).start()

    @pl.loop(0, WINDOWS + LAG_0)
    def _(i):
        @pl.when(i < WINDOWS)
        def _():
            make_gated(i)

        for piece, at, blocks in ((0, LAG_2, (2,)), (2, LAG_1, ()), (3, LAG_0, (0,))):

            @pl.when(i == at)
            def _():
                have_weight(piece)
                for block in blocks:
                    have_near_weight(block)

        @pl.when(i == 1)
        def _():
            @pl.loop(0, TILES)
            def _(tile):
                convolve(tile, ((0, tile),), query, EARLY, STEPS // 8)

        @pl.when((i >= LAG_2) & (i < WINDOWS + LAG_2))
        def _():
            w = i - LAG_2
            arrived(gated.at[w, :, pl.ds(0, 2 * WIDTH)], gs_sem.at[w])
            opposite(w)

            @pl.when(w == 0)
            def _():
                have_weight(1)
                have_near_weight(1)
                have_near_weight(3)

            sides_own(w)

        @pl.when((i >= LAG_1) & (i < WINDOWS + LAG_1))
        def _():
            sides_relayed(i - LAG_1)

        @pl.when(i >= LAG_0)
        def _():
            finish(i - LAG_0)

        @pl.when((i >= LAG_F) & (i < WINDOWS + LAG_F))
        def _():
            forward(i - LAG_F).start()

        for piece, at in ((2, 2), (3, 4)):

            @pl.when(i == at)
            def _():
                pass_weight(piece)

    left(halo, HALO)
    left(totals.at[pl.ds(1, SEQ - 1)], STATE)
    for kind in (WSIB, WZ, WX):
        left(wbuf.at[0], kind)
    left(gated.at[:, :, pl.ds(0, WIDTH)], NEAR)
    left(gated.at[:, :, pl.ds(0, 2 * WIDTH)], SIB)
    left(relay_out, RELAY)
    left(side_out, SIDE)
    pltpu.make_async_copy(result, result, result_sem.at[0]).wait()


def on_device(streams, short_taps, rates, residues, out_weight):
    gains = residues * jnp.sqrt(-jnp.expm1(-2.0 * rates))
    dma = pltpu.SemaphoreType.DMA
    hbm = pl.BlockSpec(memory_space=pl.ANY)
    result = pl.pallas_call(
        kernel,
        out_shape=jax.ShapeDtypeStruct((CHUNKS, STEPS, WIDTH), BF16),
        in_specs=[hbm] * 5,
        out_specs=hbm,
        scratch_shapes=[
            pltpu.VMEM((3, TAPS, WIDTH), F32),
            pltpu.VMEM((MODES, WIDTH), F32),
            pltpu.VMEM((MODES, WIDTH), F32),
            pltpu.VMEM((3, ROWS, WIDTH), BF16),
            pltpu.VMEM((3, 16, WIDTH), BF16),
            pltpu.VMEM((2 * TILES, CHUNKS * PITCH, LANES), F32),
            pltpu.VMEM((TILES, ROWS, LANES), F32),
            pltpu.VMEM((TILES, ROWS, LANES), F32),
            pltpu.VMEM((TILES, MODES, CHUNKS, LANES), F32),
            pltpu.VMEM((TILES, MODES, CHUNKS, LANES), F32),
            pltpu.VMEM((TILES, MODES, CHUNKS, LANES), F32),
            pltpu.VMEM((MODES, WIDTH), F32),
            pltpu.VMEM((SEQ, MODES, WIDTH), F32),
            pltpu.VMEM((CHUNKS * SPITCH, LANES), F32),
            pltpu.VMEM((WINDOWS, WROWS, 4 * WIDTH), BF16),
            pltpu.VMEM((4, 4, WIDTH, WIDTH), BF16),
            pltpu.VMEM((2, WINDOWS, WROWS, HALF), BF16),
            pltpu.VMEM((2, WINDOWS, WROWS, HALF), BF16),
            pltpu.VMEM((2, WINDOWS, 2, WROWS, HALF), BF16),
            pltpu.VMEM((2, WINDOWS, 2, WROWS, HALF), BF16),
            pltpu.VMEM((WINDOWS, CHUNKS, WSTEPS, WIDTH), BF16),
            dma((3,)),
            dma((3, TILES)),
            dma((9,)),
            dma((4,)),
            dma((1,)),
            dma((SEQ,)),
            dma((4,)),
            dma((4,)),
            dma((4,)),
            dma((WINDOWS,)),
            dma((WINDOWS,)),
            dma((WINDOWS,)),
            dma((WINDOWS,)),
            dma((1,)),
        ],
        compiler_params=pltpu.CompilerParams(
            collective_id=0, has_side_effects=True, vmem_limit_bytes=60 * 1024 * 1024
        ),
        cost_estimate=pl.CostEstimate(
            flops=2 * ROWS * WIDTH * 8192, bytes_accessed=16 * 1024 * 1024, transcendentals=0
        ),
        name="mixer",
    )(streams, short_taps, rates.T, gains.T, out_weight)
    return result.reshape(ROWS, WIDTH)


def solution(mesh):
    return jax.shard_map(
        on_device,
        mesh=mesh,
        in_specs=(
            P(None, "seq", "chan"),
            P(None, None, "chan"),
            P("chan", None),
            P("chan", None),
            P("chan", None),
        ),
        out_specs=P("seq", "chan"),
        check_vma=False,
    )
```

time: 131 us -> 117 us (0.89)
  Pallas kernels: 126 us -> 112 us
    pallas_call x1, Pallas kernels: 126 us -> 112 us  [on_device(): pl.pallas_call(kernel, out_shape=jax.ShapeDtypeStruct((CHUNKS, STEPS, WID...]
where the time goes in v2:
time: 117 us
  Pallas kernels  112 us (96%)
  local copies, waits for them, and re-layouts  3.05 us (3%)
  other arithmetic  1.42 us (1%)
    pallas_call x1, Pallas kernels, on_device(): pl.pallas_call(kernel, out_shape=jax.ShapeDtypeStruct((CHUNKS, STEPS, WID...  112 us
    unnamed x1, local copies, waits for them, and re-layouts  3.05 us

profile of v2, /device:TPU:1, one launch (start us, length us, event | category | flops | bytes accessed | tf_op | source)
XLA Modules:
  0.0 116.7 jit_solution(5850293525562631023)
XLA Ops:
  0.0 1.4 %multiply_bitcast_fusion.gains_in = f32[16,512]{1,0:T(8,128)} fusion(f32[512,16]{0,1:T(8,128)} %param.8, f32[512,16]{0,1:T(8,128)} %param.7), kind=kLoop, calls=%fused_computation | loop fusion | flops 24576 | bytes 98304 | tf_op jit(solution)/shard_map/transpose | solution.py:511
  1.4 112.2 %mixer.1 = bf16[8,256,512]{2,1,0:T(8,128)(2,1)} custom-call(bf16[3,2048,512]{2,1,0:T(8,128)(2,1)} %streams.1, f32[3,7,512]{2,1,0:T(8,128)} %taps_in.1, f32[16,512]{1,0:T(8,128)} %bitcast.5, f32[16,512]{1,0:T(8,128)} %multiply_bitcast_fusion.gains_in, bf16[512,8192]{1,0:T(8,128)(2,1)} %weight.1), custom_call_target="tpu_custom_call" | custom-call | flops 17179869184 | bytes 16777216 | tf_op jit(solution)/shard_map/mixer/pallas_call | solution.py:462
  113.6 3.0 %copy.7 = bf16[2048,512]{1,0:T(8,128)(2,1)} copy(bf16[2048,512]{1,0:T(8,128)(2,1)} %bitcast.4) | data formatting | bytes 4194304

commit v3 on v2

--- a/solution.py
+++ b/solution.py
@@ -32,12 +32,12 @@
 SEQ = 8
 XPART = WIDTH // 4
 
-LAG_F, LAG_2, LAG_1, LAG_0 = 2, 3, 5, 8
+LAG_F, LAG_2, LAG_1, LAG_0 = 2, 3, 7, 11
 
 
 def kernel(
-    streams, taps_in, rates_in, gains_in, weight, out,
-    taps, rates, gains,
+    streams, taps_in, rates_in, residues_in, weight, out,
+    taps, rates, residues,
     sbuf, halo, nat, prod, query, state, decay, gain, total, totals, stage,
     gated, wbuf, relay_out, relay_in, side_out, side_in, result,
     small_sem, load_sem, out_sem, wown_sem, halo_sem, state_sem, wsib_sem, wz_sem, wx_sem,
@@ -67,7 +67,7 @@
     x_down = (lax.rem(seq + 6, SEQ), chan)
     seq_of = lambda k: (lax.rem(seq + k, SEQ), chan)
 
-    (HALO, STATE, WSIB, WZ, WX, NEAR, SIB, RELAY, SIDE) = range(9)
+    (HALO, WSIB, WZ, WX, NEAR, SIB, RELAY, SIDE) = range(8)
 
     def send(src, dst, kind, sem, device):
         return pltpu.make_async_remote_copy(
@@ -83,7 +83,7 @@
 
     small = [
         pltpu.make_async_copy(a, b, small_sem.at[i])
-        for i, (a, b) in enumerate(((rates_in, rates), (gains_in, gains), (taps_in, taps)))
+        for i, (a, b) in enumerate(((rates_in, rates), (residues_in, residues), (taps_in, taps)))
     ]
 
     def load(j, tile):
@@ -162,10 +162,13 @@
 
     @pl.loop(0, TILES)
     def _(tile):
+        rate = rates[:, lanes_of(tile)]
+        slope = jnp.tanh(rate)
+        scale = residues[:, lanes_of(tile)] * jnp.sqrt(2.0 * slope / (1.0 + slope))
+        kept = jnp.exp(-rate)
         for m in range(MODES):
-            rate = rates[pl.ds(m, 1), lanes_of(tile)]
-            decay[tile, m] = jnp.broadcast_to(jnp.exp(-rate), (CHUNKS, LANES))
-            gain[tile, m] = jnp.broadcast_to(gains[pl.ds(m, 1), lanes_of(tile)], (CHUNKS, LANES))
+            decay[tile, m] = jnp.broadcast_to(kept[m : m + 1], (CHUNKS, LANES))
+            gain[tile, m] = jnp.broadcast_to(scale[m : m + 1], (CHUNKS, LANES))
 
     first = jnp.where(seq > 0, 1.0, 0.0).astype(F32)
 
@@ -243,6 +246,19 @@
         edge(2, tile, 2 * tile + 1)
         convolve(tile, ((1, 2 * tile), (2, 2 * tile + 1)), prod, 0, 1)
 
+    def state_copy(k, tiles):
+        return pltpu.make_async_remote_copy(
+            src_ref=total.at[tiles], dst_ref=totals.at[k, tiles],
+            send_sem=state_sem.at[0, k], recv_sem=state_sem.at[1, k],
+            device_id=seq_of(k), device_id_type=MESH,
+        )
+
+    for k in range(1, SEQ):
+
+        @pl.when(seq < k)
+        def _():
+            totals[k] = jnp.zeros((TILES, MODES, LANES), F32)
+
     sublane = lax.broadcasted_iota(jnp.int32, (CHUNKS, LANES), 0)
 
     @pl.loop(0, TILES)
@@ -266,18 +282,18 @@
                 moved = jnp.where(sublane >= shift, pltpu.roll(run, shift, 0), 0.0)
                 run = run + jnp.exp(-rate * float(STEPS * shift)) * moved
             state[tile, m] = jnp.where(sublane >= 1, pltpu.roll(run, 1, 0), 0.0)
-            total[pl.ds(m, 1), lanes_of(tile)] = run[CHUNKS - 1 :]
+            total[tile, pl.ds(m, 1)] = run[CHUNKS - 1 :]
+
+        for k in range(1, SEQ):
+
+            @pl.when(seq + k < SEQ)
+            def _():
+                state_copy(k, pl.ds(tile, 1)).start()
 
         @pl.when(tile == 0)
         def _():
             pass_weight(0)
 
-        @pl.when(tile == 1)
-        def _():
-            start_weight(2)
-
-    for k in range(1, SEQ):
-        send(total, totals.at[k], STATE, state_sem.at[k], seq_of(k)).start()
 
     @pl.loop(0, TILES)
     def _(tile):
@@ -286,23 +302,26 @@
         edge(0, tile, tile)
         convolve(tile, ((0, tile),), query, 0, EARLY)
 
+    start_weight(2)
     pass_weight(1)
-    start_weight(3)
     for k in range(1, SEQ):
-        arrived(totals.at[k], state_sem.at[k])
+
+        @pl.when(seq >= k)
+        def _():
+            state_copy(k, pl.ds(0, TILES)).wait_recv()
 
     @pl.loop(0, TILES)
     def _(tile):
-        lanes = lanes_of(tile)
-        rate = rates[:, lanes]
+        rate = rates[:, lanes_of(tile)]
         start = jnp.zeros((MODES, LANES), F32)
         for k in range(1, SEQ):
-            part = jnp.exp(-rate * float(ROWS * (k - 1))) * totals[k, :, lanes]
+            part = jnp.exp(-rate * float(ROWS * (k - 1))) * totals[k, tile]
             start = start + jnp.where(seq >= k, part, 0.0)
         for m in range(MODES):
             spread = jnp.broadcast_to(rate[m : m + 1], (CHUNKS, LANES)) * (sublane * STEPS).astype(F32)
             state[tile, m] = state[tile, m] + jnp.exp(-spread) * start[m : m + 1]
 
+    start_weight(3)
     def own_lanes():
         return pl.ds(pl.multiple_of(mine * WIDTH, WIDTH), WIDTH)
 
@@ -438,14 +457,19 @@
         def _():
             forward(i - LAG_F).start()
 
-        for piece, at in ((2, 2), (3, 4)):
+        for piece, at in ((2, 4), (3, 8)):
 
             @pl.when(i == at)
             def _():
                 pass_weight(piece)
 
     left(halo, HALO)
-    left(totals.at[pl.ds(1, SEQ - 1)], STATE)
+    for k in range(1, SEQ):
+
+        @pl.when(seq + k < SEQ)
+        def _():
+            state_copy(k, pl.ds(0, TILES)).wait_send()
+
     for kind in (WSIB, WZ, WX):
         left(wbuf.at[0], kind)
     left(gated.at[:, :, pl.ds(0, WIDTH)], NEAR)
@@ -456,7 +480,6 @@
 
 
 def on_device(streams, short_taps, rates, residues, out_weight):
-    gains = residues * jnp.sqrt(-jnp.expm1(-2.0 * rates))
     dma = pltpu.SemaphoreType.DMA
     hbm = pl.BlockSpec(memory_space=pl.ANY)
     result = pl.pallas_call(
@@ -476,8 +499,8 @@
             pltpu.VMEM((TILES, MODES, CHUNKS, LANES), F32),
             pltpu.VMEM((TILES, MODES, CHUNKS, LANES), F32),
             pltpu.VMEM((TILES, MODES, CHUNKS, LANES), F32),
-            pltpu.VMEM((MODES, WIDTH), F32),
-            pltpu.VMEM((SEQ, MODES, WIDTH), F32),
+            pltpu.VMEM((TILES, MODES, LANES), F32),
+            pltpu.VMEM((SEQ, TILES, MODES, LANES), F32),
             pltpu.VMEM((CHUNKS * SPITCH, LANES), F32),
             pltpu.VMEM((WINDOWS, WROWS, 4 * WIDTH), BF16),
             pltpu.VMEM((4, 4, WIDTH, WIDTH), BF16),
@@ -488,10 +511,10 @@
             pltpu.VMEM((WINDOWS, CHUNKS, WSTEPS, WIDTH), BF16),
             dma((3,)),
             dma((3, TILES)),
-            dma((9,)),
+            dma((8,)),
             dma((4,)),
             dma((1,)),
-            dma((SEQ,)),
+            dma((2, SEQ)),
             dma((4,)),
             dma((4,)),
             dma((4,)),
@@ -508,7 +531,7 @@
             flops=2 * ROWS * WIDTH * 8192, bytes_accessed=16 * 1024 * 1024, transcendentals=0
         ),
         name="mixer",
-    )(streams, short_taps, rates.T, gains.T, out_weight)
+    )(streams, short_taps, rates.T, residues.T, out_weight)
     return result.reshape(ROWS, WIDTH)
 
 

time: 117 us -> 110 us (0.940)
  Pallas kernels: 112 us -> 106 us
  other arithmetic: 1.42 us -> 0 us
    pallas_call x1, Pallas kernels: 112 us -> 106 us  [on_device(): pl.pallas_call(kernel, out_shape=jax.ShapeDtypeStruct((CHUNKS, STEPS, WID...]
    transpose x1 -> x0, other arithmetic: 1.42 us -> none  [on_device(): result = pl.pallas_call(kernel, out_shape=jax.ShapeDtypeStruct((CHUNKS, S...]
where the time goes in v3:
time: 110 us; the launch traced here: 109 us
  Pallas kernels  106 us (96%)
  local copies, waits for them, and re-layouts  3.05 us (3%)
    pallas_call x1, Pallas kernels, on_device(): pl.pallas_call(kernel, out_shape=jax.ShapeDtypeStruct((CHUNKS, STEPS, WID...  106 us
    unnamed x1, local copies, waits for them, and re-layouts  3.05 us

profile of v3, /device:TPU:1, one launch (start us, length us, event | category | flops | bytes accessed | tf_op | source)
XLA Modules:
  0.0 109.5 jit_solution(234927393018541091)
XLA Ops:
  0.0 106.4 %mixer.1 = bf16[8,256,512]{2,1,0:T(8,128)(2,1)} custom-call(bf16[3,2048,512]{2,1,0:T(8,128)(2,1)} %streams.1, f32[3,7,512]{2,1,0:T(8,128)} %taps_in.1, f32[16,512]{1,0:T(8,128)} %bitcast.4, f32[16,512]{1,0:T(8,128)} %bitcast.5, bf16[512,8192]{1,0:T(8,128)(2,1)} %weight.1), custom_call_target="tpu_custom_call" | custom-call | flops 17179869184 | bytes 16777216 | tf_op jit(solution)/shard_map/mixer/pallas_call | solution.py:485
  106.4 3.0 %copy.7 = bf16[2048,512]{1,0:T(8,128)(2,1)} copy(bf16[2048,512]{1,0:T(8,128)(2,1)} %bitcast.3) | data formatting | bytes 4194304

commit v4 on v3

--- a/solution.py
+++ b/solution.py
@@ -24,7 +24,8 @@
 WROWS = ROWS // WINDOWS
 HALF = WIDTH // 2
 UNROLL = 16
-EARLY = 8
+SPAN = 512
+EARLY = 4
 PAD = 8
 PITCH = STEPS + PAD
 SPITCH = WSTEPS + PAD
@@ -32,7 +33,7 @@
 SEQ = 8
 XPART = WIDTH // 4
 
-LAG_F, LAG_2, LAG_1, LAG_0 = 2, 3, 7, 11
+LAG_F, LAG_2, LAG_1, LAG_0 = 2, 3, 9, 13
 
 
 def kernel(
@@ -201,12 +202,12 @@
 
     def convolve(tile, pairs, target, first_group, groups):
         coefs = [coefs_of(j, tile) for j, _ in pairs]
-        before = [tuple(across(slot, first_group * 8 - i) for i in range(1, TAPS)) for _, slot in pairs]
+        before = [tuple(across(slot, first_group * UNROLL - i) for i in range(1, TAPS)) for _, slot in pairs]
 
         def body(g, before):
             before = list(before)
-            for u in range(8):
-                step = g * 8 + u
+            for u in range(UNROLL):
+                step = g * UNROLL + u
                 value = None
                 for k, (_, slot) in enumerate(pairs):
                     window = (across(slot, step), *before[k])
@@ -227,7 +228,7 @@
 
         for slot in range(2):
             nat[2 * tile + slot, pl.ds(0, PAD)] = jnp.zeros((PAD, LANES), F32)
-        convolve(tile, ((1, 2 * tile), (2, 2 * tile + 1)), prod, 0, STEPS // 8)
+        convolve(tile, ((1, 2 * tile), (2, 2 * tile + 1)), prod, 0, STEPS // UNROLL)
 
         @pl.when(tile == 2)
         def _():
@@ -267,14 +268,14 @@
 
         def body(g, states):
             states = list(states)
-            for u in range(8):
-                step = pl.multiple_of((g * 8 + u) * CHUNKS, CHUNKS)
+            for u in range(UNROLL):
+                step = pl.multiple_of((g * UNROLL + u) * CHUNKS, CHUNKS)
                 value = prod[tile, pl.ds(step, CHUNKS)]
                 states = [a * s + value for a, s in zip(decays, states)]
             return tuple(states)
 
         zero = jnp.zeros((CHUNKS, LANES), F32)
-        ends = lax.fori_loop(0, STEPS // 8, body, (zero,) * MODES)
+        ends = lax.fori_loop(0, STEPS // UNROLL, body, (zero,) * MODES)
         for m in range(MODES):
             rate = jnp.broadcast_to(rates[pl.ds(m, 1), lanes_of(tile)], (CHUNKS, LANES))
             run = ends[m]
@@ -429,7 +430,7 @@
         def _():
             @pl.loop(0, TILES)
             def _(tile):
-                convolve(tile, ((0, tile),), query, EARLY, STEPS // 8)
+                convolve(tile, ((0, tile),), query, EARLY, STEPS // UNROLL)
 
         @pl.when((i >= LAG_2) & (i < WINDOWS + LAG_2))
         def _():
@@ -457,7 +458,7 @@
         def _():
             forward(i - LAG_F).start()
 
-        for piece, at in ((2, 4), (3, 8)):
+        for piece, at in ((2, 5), (3, 9)):
 
             @pl.when(i == at)
             def _():
@@ -477,6 +478,22 @@
     left(relay_out, RELAY)
     left(side_out, SIDE)
     pltpu.make_async_copy(result, result, result_sem.at[0]).wait()
+
+
+def hand_on(source, target, buffer, sems):
+    def part(i, into):
+        rows = pl.ds(i * SPAN, SPAN)
+        if into:
+            return pltpu.make_async_copy(source.at[rows], buffer.at[rows], sems.at[0, i])
+        return pltpu.make_async_copy(buffer.at[rows], target.at[rows], sems.at[1, i])
+
+    for i in range(ROWS // SPAN):
+        part(i, True).start()
+    for i in range(ROWS // SPAN):
+        part(i, True).wait()
+        part(i, False).start()
+    for i in range(ROWS // SPAN):
+        part(i, False).wait()
 
 
 def on_device(streams, short_taps, rates, residues, out_weight):
@@ -532,7 +549,15 @@
         ),
         name="mixer",
     )(streams, short_taps, rates.T, residues.T, out_weight)
-    return result.reshape(ROWS, WIDTH)
+    return pl.pallas_call(
+        hand_on,
+        out_shape=jax.ShapeDtypeStruct((ROWS, WIDTH), BF16),
+        in_specs=[hbm],
+        out_specs=hbm,
+        scratch_shapes=[pltpu.VMEM((ROWS, WIDTH), BF16), dma((2, ROWS // SPAN))],
+        cost_estimate=pl.CostEstimate(flops=0, bytes_accessed=4 * ROWS * WIDTH, transcendentals=0),
+        name="hand_on",
+    )(result.reshape(ROWS, WIDTH))
 
 
 def solution(mesh):

time: 110 us -> 107 us (0.973)
  local copies, waits for them, and re-layouts: 3.05 us -> 0 us
    unnamed x1 -> x0, local copies, waits for them, and re-layouts: 3.05 us -> none
    pallas_call x1, Pallas kernels: 106 us -> 103 us  [on_device(): pl.pallas_call(kernel, out_shape=jax.ShapeDtypeStruct((CHUNKS, STEPS, WID...]
    pallas_call x0 -> x1, Pallas kernels: none -> 2.42 us  [on_device(): pl.pallas_call(hand_on, out_shape=jax.ShapeDtypeStruct((ROWS, WIDTH), BF1...]
where the time goes in v4:
time: 107 us; the launch traced here: 106 us
  Pallas kernels  106 us (99%)
    pallas_call x1, Pallas kernels, on_device(): pl.pallas_call(kernel, out_shape=jax.ShapeDtypeStruct((CHUNKS, STEPS, WID...  103 us
    pallas_call x1, Pallas kernels, on_device(): pl.pallas_call(hand_on, out_shape=jax.ShapeDtypeStruct((ROWS, WIDTH), BF1...  2.42 us

profile of v4, /device:TPU:1, one launch (start us, length us, event | category | flops | bytes accessed | tf_op | source)
XLA Modules:
  0.0 105.9 jit_solution(4677659306076100424)
XLA Ops:
  0.0 103.4 %mixer.1 = bf16[8,256,512]{2,1,0:T(8,128)(2,1)} custom-call(bf16[3,2048,512]{2,1,0:T(8,128)(2,1)} %streams.1, f32[3,7,512]{2,1,0:T(8,128)} %taps_in.1, f32[16,512]{1,0:T(8,128)} %bitcast.4, f32[16,512]{1,0:T(8,128)} %bitcast.5, bf16[512,8192]{1,0:T(8,128)(2,1)} %weight.1), custom_call_target="tpu_custom_call" | custom-call | flops 17179869184 | bytes 16777216 | tf_op jit(solution)/shard_map/mixer/pallas_call | solution.py:502
  103.5 2.4 %hand_on.1 = bf16[2048,512]{1,0:T(8,128)(2,1)} custom-call(bf16[2048,512]{1,0:T(8,128)(2,1)} %bitcast.3), custom_call_target="tpu_custom_call" | custom-call | bytes 4194304 | tf_op jit(solution)/shard_map/hand_on/pallas_call | solution.py:552

commit v5 on v4

--- a/solution.py
+++ b/solution.py
@@ -29,7 +29,7 @@
 PAD = 8
 PITCH = STEPS + PAD
 SPITCH = WSTEPS + PAD
-PIECES = (((2, None),), ((1, 1), (3, 0)), ((1, 0), (3, 1)), ((0, None),))
+PIECES = (((2, 0),), ((2, 1),), ((1, 1), (3, 0)), ((1, 0), (3, 1)), ((0, None),))
 SEQ = 8
 XPART = WIDTH // 4
 
@@ -123,10 +123,13 @@
     def part_rows(part):
         return pl.ds(pl.multiple_of(part * XPART, XPART), XPART)
 
+    def piece_rows(piece):
+        return HALF if piece < 2 else WIDTH
+
     def start_weight(piece):
         for block, n in PIECES[piece]:
             for link in range(2):
-                chip = near if link == 1 and piece < 2 else z_far
+                chip = near if link == 1 and piece < 3 else z_far
                 for c in range(2):
                     send(
                         weight.at[part_rows(pair + link), columns(block, n, 1 - zl, c)],
@@ -135,14 +138,14 @@
                     ).start()
 
     def pass_weight(piece):
-        arrived(wbuf.at[0, 0], wz_sem.at[piece])
+        arrived(wbuf.at[0, 0, pl.ds(0, piece_rows(piece))], wz_sem.at[piece])
         for block, n in PIECES[piece]:
             for way, device in enumerate((x_up, x_down)):
                 there = wbuf.at[block, far_sources, part_rows(pair + way), half(n)]
                 send(there, there, WX, wx_sem.at[piece], device).start()
 
     def have_weight(piece):
-        arrived(wbuf.at[0, 0], wx_sem.at[piece])
+        arrived(wbuf.at[0, 0, pl.ds(0, piece_rows(piece))], wx_sem.at[piece])
 
     def near_weight(block):
         there = wbuf.at[block, mine]
@@ -230,9 +233,17 @@
             nat[2 * tile + slot, pl.ds(0, PAD)] = jnp.zeros((PAD, LANES), F32)
         convolve(tile, ((1, 2 * tile), (2, 2 * tile + 1)), prod, 0, STEPS // UNROLL)
 
+        @pl.when(tile == 0)
+        def _():
+            start_weight(1)
+
         @pl.when(tile == 2)
         def _():
-            start_weight(1)
+            pass_weight(0)
+
+        @pl.when(tile == 2)
+        def _():
+            start_weight(2)
             for block in (2, 1, 3, 0):
                 near_weight(block).start()
                 own_weight(block).start()
@@ -293,7 +304,7 @@
 
         @pl.when(tile == 0)
         def _():
-            pass_weight(0)
+            pass_weight(1)
 
 
     @pl.loop(0, TILES)
@@ -303,8 +314,8 @@
         edge(0, tile, tile)
         convolve(tile, ((0, tile),), query, 0, EARLY)
 
-    start_weight(2)
-    pass_weight(1)
+    start_weight(3)
+    pass_weight(2)
     for k in range(1, SEQ):
 
         @pl.when(seq >= k)
@@ -322,7 +333,7 @@
             spread = jnp.broadcast_to(rate[m : m + 1], (CHUNKS, LANES)) * (sublane * STEPS).astype(F32)
             state[tile, m] = state[tile, m] + jnp.exp(-spread) * start[m : m + 1]
 
-    start_weight(3)
+    start_weight(4)
     def own_lanes():
         return pl.ds(pl.multiple_of(mine * WIDTH, WIDTH), WIDTH)
 
@@ -418,7 +429,7 @@
         def _():
             make_gated(i)
 
-        for piece, at, blocks in ((0, LAG_2, (2,)), (2, LAG_1, ()), (3, LAG_0, (0,))):
+        for piece, at, blocks in ((0, LAG_2, ()), (1, LAG_2, (2,)), (3, LAG_1, ()), (4, LAG_0, (0,))):
 
             @pl.when(i == at)
             def _():
@@ -440,7 +451,7 @@
 
             @pl.when(w == 0)
             def _():
-                have_weight(1)
+                have_weight(2)
                 have_near_weight(1)
                 have_near_weight(3)
 
@@ -458,7 +469,7 @@
         def _():
             forward(i - LAG_F).start()
 
-        for piece, at in ((2, 5), (3, 9)):
+        for piece, at in ((3, 5), (4, 9)):
 
             @pl.when(i == at)
             def _():
@@ -533,8 +544,8 @@
             dma((1,)),
             dma((2, SEQ)),
             dma((4,)),
-            dma((4,)),
-            dma((4,)),
+            dma((5,)),
+            dma((5,)),
             dma((WINDOWS,)),
             dma((WINDOWS,)),
             dma((WINDOWS,)),

time: 107 us -> 106 us (level)
  no operation moved by 1% of the time
where the time goes in v5:
time: 106 us; the launch traced here: 105 us
  Pallas kernels  105 us (99%)
    pallas_call x1, Pallas kernels, on_device(): pl.pallas_call(kernel, out_shape=jax.ShapeDtypeStruct((CHUNKS, STEPS, WID...  103 us
    pallas_call x1, Pallas kernels, on_device(): pl.pallas_call(hand_on, out_shape=jax.ShapeDtypeStruct((ROWS, WIDTH), BF1...  2.42 us

profile of v5, /device:TPU:1, one launch (start us, length us, event | category | flops | bytes accessed | tf_op | source)
XLA Modules:
  0.0 105.1 jit_solution(5411513893193624235)
XLA Ops:
  0.0 102.6 %mixer.1 = bf16[8,256,512]{2,1,0:T(8,128)(2,1)} custom-call(bf16[3,2048,512]{2,1,0:T(8,128)(2,1)} %streams.1, f32[3,7,512]{2,1,0:T(8,128)} %taps_in.1, f32[16,512]{1,0:T(8,128)} %bitcast.4, f32[16,512]{1,0:T(8,128)} %bitcast.5, bf16[512,8192]{1,0:T(8,128)(2,1)} %weight.1), custom_call_target="tpu_custom_call" | custom-call | flops 17179869184 | bytes 16777216 | tf_op jit(solution)/shard_map/mixer/pallas_call | solution.py:513
  102.6 2.4 %hand_on.1 = bf16[2048,512]{1,0:T(8,128)(2,1)} custom-call(bf16[2048,512]{1,0:T(8,128)(2,1)} %bitcast.3), custom_call_target="tpu_custom_call" | custom-call | bytes 4194304 | tf_op jit(solution)/shard_map/hand_on/pallas_call | solution.py:563

commit v6 on v5

--- a/solution.py
+++ b/solution.py
@@ -521,7 +521,7 @@
             pltpu.VMEM((MODES, WIDTH), F32),
             pltpu.VMEM((3, ROWS, WIDTH), BF16),
             pltpu.VMEM((3, 16, WIDTH), BF16),
-            pltpu.VMEM((2 * TILES, CHUNKS * PITCH, LANES), F32),
+            pltpu.VMEM((2 * TILES, (CHUNKS + 1) * PITCH, LANES), F32),
             pltpu.VMEM((TILES, ROWS, LANES), F32),
             pltpu.VMEM((TILES, ROWS, LANES), F32),
             pltpu.VMEM((TILES, MODES, CHUNKS, LANES), F32),
@@ -529,7 +529,7 @@
             pltpu.VMEM((TILES, MODES, CHUNKS, LANES), F32),
             pltpu.VMEM((TILES, MODES, LANES), F32),
             pltpu.VMEM((SEQ, TILES, MODES, LANES), F32),
-            pltpu.VMEM((CHUNKS * SPITCH, LANES), F32),
+            pltpu.VMEM(((CHUNKS + 1) * SPITCH, LANES), F32),
             pltpu.VMEM((WINDOWS, WROWS, 4 * WIDTH), BF16),
             pltpu.VMEM((4, 4, WIDTH, WIDTH), BF16),
             pltpu.VMEM((2, WINDOWS, WROWS, HALF), BF16),

time: 106 us -> 106 us (level)
  no operation moved by 1% of the time
where the time goes in v6:
time: 106 us; the launch traced here: 105 us
  Pallas kernels  105 us (99%)
    pallas_call x1, Pallas kernels, on_device(): pl.pallas_call(kernel, out_shape=jax.ShapeDtypeStruct((CHUNKS, STEPS, WID...  103 us
    pallas_call x1, Pallas kernels, on_device(): pl.pallas_call(hand_on, out_shape=jax.ShapeDtypeStruct((ROWS, WIDTH), BF1...  2.42 us

profile of v6, /device:TPU:1, one launch (start us, length us, event | category | flops | bytes accessed | tf_op | source)
XLA Modules:
  0.0 105.1 jit_solution(18347143154316893329)
XLA Ops:
  0.0 102.7 %mixer.1 = bf16[8,256,512]{2,1,0:T(8,128)(2,1)} custom-call(bf16[3,2048,512]{2,1,0:T(8,128)(2,1)} %streams.1, f32[3,7,512]{2,1,0:T(8,128)} %taps_in.1, f32[16,512]{1,0:T(8,128)} %bitcast.4, f32[16,512]{1,0:T(8,128)} %bitcast.5, bf16[512,8192]{1,0:T(8,128)(2,1)} %weight.1), custom_call_target="tpu_custom_call" | custom-call | flops 17179869184 | bytes 16777216 | tf_op jit(solution)/shard_map/mixer/pallas_call | solution.py:513
  102.7 2.4 %hand_on.1 = bf16[2048,512]{1,0:T(8,128)(2,1)} custom-call(bf16[2048,512]{1,0:T(8,128)(2,1)} %bitcast.3), custom_call_target="tpu_custom_call" | custom-call | bytes 4194304 | tf_op jit(solution)/shard_map/hand_on/pallas_call | solution.py:563
